TPU v7x, 32 devices: a whole 2x2x4 slice. The times are simulated.
32 devices in a mesh: seq: 8 (over z, core), tensor: 4 (over y, x).
Axes of the slice: x: 2, y: 2, z: 4, core: 2. Of those that a mesh axis runs over, the one named last changes fastest.
Arguments:
- tokens: bfloat16 [1024, 8192], P('seq', 'tensor'), may hold values from -2000 to 2000
- cotangent: bfloat16 [1024, 8192], P('seq', 'tensor'), may hold values from -6 to 6
- gain: float32 [8192], P('tensor'), may hold values from 0.25 to 1.75
- w_gate: bfloat16 [8192, 14336], P('tensor', 'seq'), may hold values from -0.0625 to 0.0625
- w_up: bfloat16 [8192, 14336], P('tensor', 'seq'), may hold values from -0.0625 to 0.0625
- w_down: bfloat16 [14336, 8192], P('seq', 'tensor'), may hold values from -0.046875 to 0.046875
- probe: bfloat16 [8192, 14336], P('tensor', 'seq'), may hold values from -1 to 1, as said below
Outputs:
- hessian_probe: float32 [8192, 14336], P('tensor', 'seq')
Inputs may be any that keep to these rules, and one draw needn't show every extreme that they name: `probe`: every entry is +1 or -1.
All inputs are finite; a program needn't handle non-finite values.
Results may differ from a plain program's by a relative error of at most 0.024.
Values may be sent and summed in bfloat16 or wider, within the bound.
A program may use at most 128 MiB of HBM per device.

v0:
```python
import functools

import jax
import jax.numpy as jnp
from jax import lax
from jax.experimental import pallas as pl
from jax.experimental.pallas import tpu as pltpu
from jax.sharding import PartitionSpec as P

epsilon = 1e-05


def second_factor(pre_gate, pre_up, tangent, upstream):
    sigmoid_gate = jax.nn.sigmoid(pre_gate)
    curvature = sigmoid_gate * (1.0 - sigmoid_gate) * (2.0 + pre_gate * (1.0 - 2.0 * sigmoid_gate))
    return (upstream * pre_up * curvature * tangent).astype(jnp.bfloat16)


def swap(value, axis, size, mask):
    return lax.ppermute(value, axis, [(i, i ^ mask) for i in range(size)])


def bit_of(bit):
    return (lax.axis_index("tensor") >> bit) & 1


def after(value, waited):
    return lax.optimization_barrier((value, waited))[0]


def scatter_sum(parts, order, size):
    bits = len(order)
    rows, width = parts[0].shape
    left = list(range(bits - 1, -1, -1))
    held = [part.reshape([2] * bits + [rows // size, width]) for part in parts]
    first = None
    for bit in order:
        place = left.index(bit)
        mine = bit_of(bit)
        sent = [lax.dynamic_index_in_dim(h, 1 - mine, place, False).astype(jnp.bfloat16) for h in held]
        if first is None:
            came = [swap(one, "tensor", size, 1 << bit) for one in sent]
        else:
            came = swap(jnp.concatenate(sent, axis=-1), "tensor", size, 1 << bit)
            came = [came[..., k * width : (k + 1) * width] for k in range(len(held))]
        first = came[0] if first is None else first
        held = [
            lax.dynamic_index_in_dim(h, mine, place, False).astype(jnp.float32)
            + c.astype(jnp.float32)
            for h, c in zip(held, came)
        ]
        left.pop(place)
    return held, first


def gather_rows(block, order, size):
    done = []
    for bit in order:
        place = sum(1 for other in done if other > bit)
        mine = bit_of(bit)
        came = swap(block, "tensor", size, 1 << bit)
        low = jnp.where(mine == 0, block, came)
        high = jnp.where(mine == 0, came, block)
        block = jnp.stack([low, high], axis=place)
        done.append(bit)
    return block.reshape(-1, block.shape[-1])


def arrival(chip, step, chips):
    both = min(chip, chips - 1 - chip)
    if step <= 2 * both:
        return ("left" if step % 2 else "right", (step + 1) // 2)
    return ("left" if chip > chips - 1 - chip else "right", step - both)


def product_kernel(scale, left_ref, right_ref, out_ref):
    out_ref[...] = jnp.dot(left_ref[...], right_ref[...], preferred_element_type=jnp.float32) * scale


def scaled_product(left, right, scale):
    rows, depth = left.shape
    width = right.shape[1]
    tile = 256
    return pl.pallas_call(
        functools.partial(product_kernel, scale),
        grid=(rows // tile,),
        in_specs=[
            pl.BlockSpec((tile, depth), lambda i: (i, 0)),
            pl.BlockSpec((depth, width), lambda i: (0, 0)),
        ],
        out_specs=pl.BlockSpec((tile, width), lambda i: (i, 0)),
        out_shape=jax.ShapeDtypeStruct((rows, width), jnp.float32),
        compiler_params=pltpu.CompilerParams(vmem_limit_bytes=32 * 1024 * 1024),
        cost_estimate=pl.CostEstimate(
            flops=2 * rows * depth * width,
            bytes_accessed=2 * depth * (rows + width) + 4 * rows * width,
            transcendentals=0,
        ),
    )(left, right)


def rows_kernel(transposed, left_ref, *refs):
    weights, outs = refs[: len(refs) // 2], refs[len(refs) // 2 :]
    for weight_ref, out_ref in zip(weights, outs):
        out_ref[...] = lax.dot_general(
            left_ref[...],
            weight_ref[...],
            (((1,), (1 if transposed else 0,)), ((), ())),
            preferred_element_type=jnp.float32,
        ).astype(out_ref.dtype)


def rows_products(left, weights, transposed):
    rows, depth = left.shape
    width = weights[0].shape[0 if transposed else 1]
    tile = 256 if width % 256 == 0 else 128
    if transposed:
        weight_spec = pl.BlockSpec((tile, depth), lambda i: (i, 0))
    else:
        weight_spec = pl.BlockSpec((depth, tile), lambda i: (0, i))
    count = len(weights)
    return pl.pallas_call(
        functools.partial(rows_kernel, transposed),
        grid=(width // tile,),
        in_specs=[pl.BlockSpec((rows, depth), lambda i: (0, 0))] + [weight_spec] * count,
        out_specs=[pl.BlockSpec((rows, tile), lambda i: (0, i))] * count,
        out_shape=[jax.ShapeDtypeStruct((rows, width), jnp.bfloat16)] * count,
        compiler_params=pltpu.CompilerParams(vmem_limit_bytes=24 * 1024 * 1024),
        cost_estimate=pl.CostEstimate(
            flops=2 * count * rows * depth * width,
            bytes_accessed=2 * (rows * depth + count * width * (rows + depth)),
            transcendentals=0,
        ),
    )(left, *weights)


def body(n_seq, n_tensor, tokens, cotangent, gain, w_gate, w_up, w_down, probe):
    chips = n_seq // 2
    bits = n_tensor.bit_length() - 1
    up_order = list(range(bits))
    down_order = up_order[::-1]
    rows = tokens.shape[0]
    features = tokens.shape[1] * n_tensor
    total_tokens = rows * n_seq

    values = tokens.astype(jnp.float32)
    squares = jnp.sum(values * values, axis=1)
    for bit in up_order:
        squares = squares + swap(squares, "tensor", n_tensor, 1 << bit)
    inverse = lax.rsqrt(squares / features + epsilon)
    normed = (values * inverse[:, None] * gain[None, :]).astype(jnp.bfloat16)

    own = jnp.concatenate([normed, cotangent], axis=0)
    rightward = [(i, i + 2) for i in range(n_seq - 2)]
    leftward = [(i + 2, i) for i in range(n_seq - 2)]
    came = {("left", 0): own, ("right", 0): own}

    def pass_on(distance, waited):
        left, right = after((came["left", distance - 1], came["right", distance - 1]), waited)
        came["left", distance] = lax.ppermute(left, "seq", rightward)
        came["right", distance] = lax.ppermute(right, "seq", leftward)

    pass_on(1, ())
    chip = lax.axis_index("seq") // 2

    def products(norm_rows, cot_rows):
        return [
            *rows_products(cot_rows, [w_down], True),
            *rows_products(norm_rows, [probe, w_gate, w_up], False),
        ]

    def gathered(one, other):
        return [gather_rows(one, up_order, n_tensor), gather_rows(other, down_order, n_tensor)]

    def gathered_alone(second):
        half = second.shape[1] // 2
        return jnp.concatenate(gathered(second[:, :half], second[:, half:]), axis=1)

    all_norm, all_second, firsts, seconds = [], [], [], []
    for step in range(chips):
        if step == 0:
            cot_rows = jnp.concatenate([cotangent, swap(cotangent, "seq", n_seq, 1)], axis=0)
            norm_rows = jnp.concatenate([normed, swap(normed, "seq", n_seq, 1)], axis=0)
        else:
            where_from = [arrival(c, step, chips) for c in range(chips)]
            kinds = sorted(set(where_from))
            candidates = after([came[kind] for kind in kinds], (firsts[step - 1], seconds[: step - 1]))
            block = candidates[0]
            for kind, candidate in zip(kinds[1:], candidates[1:]):
                for c in range(chips):
                    if where_from[c] == kind:
                        block = jnp.where(chip == c, candidate, block)
            other = swap(block, "seq", n_seq, 1)
            norm_rows = jnp.concatenate([block[:rows], other[:rows]], axis=0)
            cot_rows = jnp.concatenate([block[rows:], other[rows:]], axis=0)
        all_norm.append(norm_rows)
        if step == chips - 1:
            norm_columns = jnp.concatenate(all_norm, axis=0).T
            cot_rows, norm_columns = lax.optimization_barrier((cot_rows, norm_columns))

        parts = products(norm_rows, cot_rows)
        if step == chips - 1:
            ready = after(seconds, parts)
            while len(ready) > 1:
                all_second += gathered(ready[0], ready[1])
                ready = ready[2:]
            all_second += [gathered_alone(one) for one in ready]
        upstream, tangent, pre_gate, pre_up = parts
        (upstream, pre_gate), first = scatter_sum([upstream, pre_gate], up_order, n_tensor)
        (tangent, pre_up), other_first = scatter_sum([tangent, pre_up], down_order, n_tensor)
        firsts.append((first, other_first))
        if step < chips - 2:
            pass_on(step + 2, (firsts[-1], seconds))
        second = second_factor(pre_gate, pre_up, tangent, upstream)
        seconds.append(second)

    all_second.append(gathered_alone(seconds[-1]))
    return scaled_product(norm_columns, jnp.concatenate(all_second, axis=0), 1.0 / total_tokens)


def solution(mesh):
    return jax.shard_map(
        functools.partial(body, mesh.shape["seq"], mesh.shape["tensor"]),
        mesh=mesh,
        in_specs=(
            P("seq", "tensor"),
            P("seq", "tensor"),
            P("tensor"),
            P("tensor", "seq"),
            P("tensor", "seq"),
            P("seq", "tensor"),
            P("tensor", "seq"),
        ),
        out_specs=P("tensor", "seq"),
        check_vma=False,
    )
```

profile of v0, /device:TPU:0, one launch (start us, length us, event | category | flops | bytes accessed | tf_op | source)
XLA Modules:
  0.0 364.9 jit_solution(14865653598847553406)
XLA Ops:
  14.8 3.4 shard_map.73
  22.8 4.6 %collective-permute-start.2 = (bf16[256,2048]{0,1:T(8,128)(2,1)}, bf16[256,2048]{0,1:T(8,128)(2,1)}, u32[]{:S(2)}, u32[]{:S(2)}) collective-permute-start(bf16[256,2048]{0,1:T(8,128)(2,1)} %get-tuple-element.36), channel_id=1, source_target_pairs={{0,8},{4,12},{8,16},{12,20},{16,24},{20,28},{1,9},{5,13},{9,17},{1... | collective-permute-start | bytes 3145736 | tf_op jit(solution)/shard_map/ppermute | solution.py:160
  34.9 3.1 copy-done.10
  38.0 8.6 %shard_map.74 = (bf16[256,1792]{1,0:T(8,128)(2,1)S(1)}, bf16[256,1792]{1,0:T(8,128)(2,1)S(1)}, bf16[256,1792]{1,0:T(8,128)(2,1)S(1)}) custom-call(bf16[256,2048]{1,0:T(8,128)(2,1)S(1)} %copy.10.left_ref, bf16[2048,1792]{1,0:T(8,128)(2,1)S(1)} %copy-done.4, bf16[2048,1792]{1,0:T(8,128)(2,1)S(1)} %copy-done.6, bf16[2048,1792]{1,0:T(8,128)(2,1)S(1)} %copy-done.10), custom_call_target="tpu_custom_call" | custom-call | flops 5637144576 | bytes 25821184 | tf_op jit(solution)/shard_map/pallas_call | solution.py:122
  50.6 9.5 %collective-permute-done.15 = bf16[2,64,1792]{2,1,0:T(8,128)(2,1)S(1)} collective-permute-done((bf16[2,64,1792]{2,1,0:T(8,128)(2,1)S(1)}, bf16[2,64,1792]{2,1,0:T(8,128)(2,1)S(1)}, u32[]{:S(2)}, u32[]{:S(2)}) %collective-permute-start.15) | collective-permute-done | bytes 458784 | tf_op jit(solution)/shard_map/ppermute | solution.py:20
  60.2 8.7 %collective-permute-done.7 = bf16[2,64,1792]{2,1,0:T(8,128)(2,1)S(1)} collective-permute-done((bf16[2,64,1792]{2,1,0:T(8,128)(2,1)S(1)}, bf16[2,64,1792]{2,1,0:T(8,128)(2,1)S(1)}, u32[]{:S(2)}, u32[]{:S(2)}) %collective-permute-start.7) | collective-permute-done | bytes 458784 | tf_op jit(solution)/shard_map/ppermute | solution.py:20
  72.5 8.1 %collective-permute-done.16 = bf16[64,3584]{1,0:T(8,128)(2,1)S(1)} collective-permute-done((bf16[64,3584]{1,0:T(8,128)(2,1)S(1)}, bf16[64,3584]{1,0:T(8,128)(2,1)S(1)}, u32[]{:S(2)}, u32[]{:S(2)}) %collective-permute-start.16) | collective-permute-done | bytes 458784 | tf_op jit(solution)/shard_map/ppermute | solution.py:20
  82.2 4.9 %collective-permute-start.8 = (bf16[256,2048]{0,1:T(8,128)(2,1)}, bf16[256,2048]{0,1:T(8,128)(2,1)}, u32[]{:S(2)}, u32[]{:S(2)}) collective-permute-start(bf16[256,2048]{0,1:T(8,128)(2,1)} %collective-permute-done.2), channel_id=1, source_target_pairs={{0,8},{4,12},{8,16},{12,20},{16,24},{20,28},{1,9},{5,13},{9,17},{1... | collective-permute-start | bytes 3145736 | tf_op jit(solution)/shard_map/ppermute | solution.py:160
  96.7 3.4 shard_map.75
  106.3 3.1 copy-done.7
  112.5 8.6 %shard_map.76 = (bf16[256,1792]{1,0:T(8,128)(2,1)S(1)}, bf16[256,1792]{1,0:T(8,128)(2,1)S(1)}, bf16[256,1792]{1,0:T(8,128)(2,1)S(1)}) custom-call(bf16[256,2048]{1,0:T(8,128)(2,1)S(1)} %copy.12.left_ref, bf16[2048,1792]{1,0:T(8,128)(2,1)S(1)} %copy-done.5, bf16[2048,1792]{1,0:T(8,128)(2,1)S(1)} %copy-done.7, bf16[2048,1792]{1,0:T(8,128)(2,1)S(1)} %copy-done.11), custom_call_target="tpu_custom_call" | custom-call | flops 5637144576 | bytes 25821184 | tf_op jit(solution)/shard_map/pallas_call | solution.py:122
  123.3 11.3 %collective-permute-done.24 = bf16[2,64,1792]{2,1,0:T(8,128)(2,1)S(1)} collective-permute-done((bf16[2,64,1792]{2,1,0:T(8,128)(2,1)S(1)}, bf16[2,64,1792]{2,1,0:T(8,128)(2,1)S(1)}, u32[]{:S(2)}, u32[]{:S(2)}) %collective-permute-start.24) | collective-permute-done | bytes 458784 | tf_op jit(solution)/shard_map/ppermute | solution.py:20
  135.4 5.1 %collective-permute-done.12 = bf16[2,64,1792]{2,1,0:T(8,128)(2,1)S(1)} collective-permute-done((bf16[2,64,1792]{2,1,0:T(8,128)(2,1)S(1)}, bf16[2,64,1792]{2,1,0:T(8,128)(2,1)S(1)}, u32[]{:S(2)}, u32[]{:S(2)}) %collective-permute-start.12) | collective-permute-done | bytes 458784 | tf_op jit(solution)/shard_map/ppermute | solution.py:20
  142.4 4.4 %collective-permute-done.22 = bf16[2,64,1792]{2,1,0:T(8,128)(2,1)S(1)} collective-permute-done((bf16[2,64,1792]{2,1,0:T(8,128)(2,1)S(1)}, bf16[2,64,1792]{2,1,0:T(8,128)(2,1)S(1)}, u32[]{:S(2)}, u32[]{:S(2)}) %collective-permute-start.22) | collective-permute-done | bytes 458784 | tf_op jit(solution)/shard_map/ppermute | solution.py:20
  150.4 4.7 %collective-permute-start.17 = (bf16[256,2048]{0,1:T(8,128)(2,1)}, bf16[256,2048]{0,1:T(8,128)(2,1)}, u32[]{:S(2)}, u32[]{:S(2)}) collective-permute-start(bf16[256,2048]{0,1:T(8,128)(2,1)} %collective-permute-done.8), channel_id=1, source_target_pairs={{0,8},{4,12},{8,16},{12,20},{16,24},{20,28},{1,9},{5,13},{9,17},{1... | collective-permute-start | bytes 3145736 | tf_op jit(solution)/shard_map/ppermute | solution.py:160
  157.8 4.0 %collective-permute-done.23 = bf16[64,3584]{1,0:T(8,128)(2,1)S(1)} collective-permute-done((bf16[64,3584]{1,0:T(8,128)(2,1)S(1)}, bf16[64,3584]{1,0:T(8,128)(2,1)S(1)}, u32[]{:S(2)}, u32[]{:S(2)}) %collective-permute-start.23) | collective-permute-done | bytes 458784 | tf_op jit(solution)/shard_map/ppermute | solution.py:20
  176.4 3.4 shard_map.77
  186.7 8.6 %shard_map.78 = (bf16[256,1792]{1,0:T(8,128)(2,1)S(1)}, bf16[256,1792]{1,0:T(8,128)(2,1)S(1)}, bf16[256,1792]{1,0:T(8,128)(2,1)S(1)}) custom-call(bf16[256,2048]{1,0:T(8,128)(2,1)S(1)} %copy-done.15, bf16[2048,1792]{1,0:T(8,128)(2,1)S(1)} %bitcast.274, bf16[2048,1792]{1,0:T(8,128)(2,1)S(1)} %copy-done.8, bf16[2048,1792]{1,0:T(8,128)(2,1)S(1)} %copy-done.12), custom_call_target="tpu_custom_call" | custom-call | flops 5637144576 | bytes 25821184 | tf_op jit(solution)/shard_map/pallas_call | solution.py:122
  197.6 11.3 %collective-permute-done.29 = bf16[2,64,1792]{2,1,0:T(8,128)(2,1)S(1)} collective-permute-done((bf16[2,64,1792]{2,1,0:T(8,128)(2,1)S(1)}, bf16[2,64,1792]{2,1,0:T(8,128)(2,1)S(1)}, u32[]{:S(2)}, u32[]{:S(2)}) %collective-permute-start.29) | collective-permute-done | bytes 458784 | tf_op jit(solution)/shard_map/ppermute | solution.py:20
  210.5 6.8 %collective-permute-done.21 = bf16[2,64,1792]{2,1,0:T(8,128)(2,1)S(1)} collective-permute-done((bf16[2,64,1792]{2,1,0:T(8,128)(2,1)S(1)}, bf16[2,64,1792]{2,1,0:T(8,128)(2,1)S(1)}, u32[]{:S(2)}, u32[]{:S(2)}) %collective-permute-start.21) | collective-permute-done | bytes 458784 | tf_op jit(solution)/shard_map/ppermute | solution.py:20
  223.9 4.7 %collective-permute-done.30 = bf16[64,3584]{1,0:T(8,128)(2,1)S(1)} collective-permute-done((bf16[64,3584]{1,0:T(8,128)(2,1)S(1)}, bf16[64,3584]{1,0:T(8,128)(2,1)S(1)}, u32[]{:S(2)}, u32[]{:S(2)}) %collective-permute-start.30) | collective-permute-done | bytes 458784 | tf_op jit(solution)/shard_map/ppermute | solution.py:20
  228.5 5.5 %collective-permute-done.28 = bf16[64,3584]{1,0:T(8,128)(2,1)S(1)} collective-permute-done((bf16[64,3584]{1,0:T(8,128)(2,1)S(1)}, bf16[64,3584]{1,0:T(8,128)(2,1)S(1)}, u32[]{:S(2)}, u32[]{:S(2)}) %collective-permute-start.28) | collective-permute-done | bytes 458784 | tf_op jit(solution)/shard_map/ppermute | solution.py:20
  248.1 3.4 shard_map.79
  258.6 8.6 %shard_map.80 = (bf16[256,1792]{1,0:T(8,128)(2,1)S(1)}, bf16[256,1792]{1,0:T(8,128)(2,1)S(1)}, bf16[256,1792]{1,0:T(8,128)(2,1)S(1)}) custom-call(bf16[256,2048]{1,0:T(8,128)(2,1)S(1)} %copy-done.14, bf16[2048,1792]{1,0:T(8,128)(2,1)S(1)} %bitcast.276, bf16[2048,1792]{1,0:T(8,128)(2,1)S(1)} %copy-done.9, bf16[2048,1792]{1,0:T(8,128)(2,1)S(1)} %copy-done.13), custom_call_target="tpu_custom_call" | custom-call | flops 5637144576 | bytes 25821184 | tf_op jit(solution)/shard_map/pallas_call | solution.py:122
  276.3 3.2 collective-permute-done.33
  281.8 12.6 %collective-permute-done.38 = bf16[2,64,896]{2,1,0:T(8,128)(2,1)S(1)} collective-permute-done((bf16[2,64,896]{2,1,0:T(8,128)(2,1)S(1)}, bf16[2,64,896]{2,1,0:T(8,128)(2,1)S(1)}, u32[]{:S(2)}, u32[]{:S(2)}) %collective-permute-start.38) | collective-permute-done | bytes 229408 | tf_op jit(solution)/shard_map/ppermute | solution.py:20
  294.9 7.9 %collective-permute-done.36 = bf16[2,64,896]{2,1,0:T(8,128)(2,1)S(1)} collective-permute-done((bf16[2,64,896]{2,1,0:T(8,128)(2,1)S(1)}, bf16[2,64,896]{2,1,0:T(8,128)(2,1)S(1)}, u32[]{:S(2)}, u32[]{:S(2)}) %collective-permute-start.36) | collective-permute-done | bytes 229408 | tf_op jit(solution)/shard_map/ppermute | solution.py:20
  307.9 8.4 %collective-permute-done.32 = bf16[2,64,1792]{2,1,0:T(8,128)(2,1)S(1)} collective-permute-done((bf16[2,64,1792]{2,1,0:T(8,128)(2,1)S(1)}, bf16[2,64,1792]{2,1,0:T(8,128)(2,1)S(1)}, u32[]{:S(2)}, u32[]{:S(2)}) %collective-permute-start.32) | collective-permute-done | bytes 458784 | tf_op jit(solution)/shard_map/ppermute | solution.py:20
  317.5 6.7 %collective-permute-done.44 = bf16[64,3584]{1,0:T(8,128)(2,1)S(1)} collective-permute-done((bf16[64,3584]{1,0:T(8,128)(2,1)S(1)}, bf16[64,3584]{1,0:T(8,128)(2,1)S(1)}, u32[]{:S(2)}, u32[]{:S(2)}) %collective-permute-start.44) | collective-permute-done | bytes 458784 | tf_op jit(solution)/shard_map/ppermute | solution.py:20
  326.9 3.3 collective-permute-done.45
  338.8 13.7 %maximum_maximum_fusion.right_ref = bf16[1024,1792]{1,0:T(8,128)(2,1)S(1)} fusion(bf16[256,896]{1,0:T(8,128)(2,1)S(1)} %bitcast.313, bf16[256,896]{1,0:T(8,128)(2,1)S(1)} %bitcast.314, bf16[256,896]{1,0:T(8,128)(2,1)S(1)} %bitcast.311, bf16[256,896]{1,0:T(8,128)(2,1)S(1)} %bitcast.312, bf16[256,1792]{1,0:T(8,128)(2,1)S(1)} %bitcast.310, ...), kind=kLoop, calls=%fused_computation | loop fusion | flops 22020096 | bytes 7340032 | tf_op jit(solution)/shard_map/concatenate | solution.py:218
  352.4 12.4 %shard_map.81 = f32[2048,1792]{1,0:T(8,128)} custom-call(bf16[2048,1024]{1,0:T(8,128)(2,1)} %bitcast.44.left_ref, bf16[1024,1792]{1,0:T(8,128)(2,1)S(1)} %maximum_maximum_fusion.right_ref), custom_call_target="tpu_custom_call" | custom-call | flops 7516192768 | bytes 22544384 | tf_op jit(solution)/shard_map/pallas_call | solution.py:84
  (244 shorter events, 148.3 us)
Async XLA Ops:
  19.1 29.8 %collective-permute-start.5 = (bf16[2,64,1792]{2,1,0:T(8,128)(2,1)}, bf16[2,64,1792]{2,1,0:T(8,128)(2,1)}, u32[]{:S(2)}, u32[]{:S(2)}) collective-permute-start(bf16[2,64,1792]{2,1,0:T(8,128)(2,1)} %dynamic-slice_bitcast_fusion.15), channel_id=1, source_target_pairs={{0,1},{1,0},{2,3},{3,2},{4,5},{5,4},{6,7},{7,6},{8,9},{9,8},{10,11... | collective-permute-start | bytes 1376264 | tf_op jit(solution)/shard_map/ppermute | solution.py:20
  22.8 48.6 %collective-permute-start.2 = (bf16[256,2048]{0,1:T(8,128)(2,1)}, bf16[256,2048]{0,1:T(8,128)(2,1)}, u32[]{:S(2)}, u32[]{:S(2)}) collective-permute-start(bf16[256,2048]{0,1:T(8,128)(2,1)} %get-tuple-element.36), channel_id=1, source_target_pairs={{0,8},{4,12},{8,16},{12,20},{16,24},{20,28},{1,9},{5,13},{9,17},{1... | collective-permute-start | bytes 3145736 | tf_op jit(solution)/shard_map/ppermute | solution.py:160
  27.4 44.0 %collective-permute-start.3 = (bf16[256,2048]{0,1:T(8,128)(2,1)}, bf16[256,2048]{0,1:T(8,128)(2,1)S(1)}, u32[]{:S(2)}, u32[]{:S(2)}) collective-permute-start(bf16[256,2048]{0,1:T(8,128)(2,1)} %get-tuple-element.36), channel_id=1, source_target_pairs={{8,0},{12,4},{16,8},{20,12},{24,16},{28,20},{9,1},{13,5},{17,9},{2... | collective-permute-start | bytes 3145736 | tf_op jit(solution)/shard_map/ppermute | solution.py:161
  46.6 13.5 %collective-permute-start.15 = (bf16[2,64,1792]{2,1,0:T(8,128)(2,1)S(1)}, bf16[2,64,1792]{2,1,0:T(8,128)(2,1)S(1)}, u32[]{:S(2)}, u32[]{:S(2)}) collective-permute-start(bf16[2,64,1792]{2,1,0:T(8,128)(2,1)S(1)} %dynamic-slice_bitcast_fusion.10), channel_id=1, source_target_pairs={{0,2},{1,3},{2,0},{3,1},{4,6},{5,7},{6,4},{7,5},{8,10},{9,11},{10,... | collective-permute-start | bytes 1376264 | tf_op jit(solution)/shard_map/ppermute | solution.py:20
  48.2 20.6 %collective-permute-start.7 = (bf16[2,64,1792]{2,1,0:T(8,128)(2,1)S(1)}, bf16[2,64,1792]{2,1,0:T(8,128)(2,1)S(1)}, u32[]{:S(2)}, u32[]{:S(2)}) collective-permute-start(bf16[2,64,1792]{2,1,0:T(8,128)(2,1)S(1)} %dynamic-slice_bitcast_fusion.14), channel_id=1, source_target_pairs={{0,2},{1,3},{2,0},{3,1},{4,6},{5,7},{6,4},{7,5},{8,10},{9,11},{10,... | collective-permute-start | bytes 1376264 | tf_op jit(solution)/shard_map/ppermute | solution.py:20
  48.9 20.8 %collective-permute-start.13 = (bf16[2,64,1792]{2,1,0:T(8,128)(2,1)S(1)}, bf16[2,64,1792]{2,1,0:T(8,128)(2,1)S(1)}, u32[]{:S(2)}, u32[]{:S(2)}) collective-permute-start(bf16[2,64,1792]{2,1,0:T(8,128)(2,1)S(1)} %dynamic-slice_bitcast_fusion.11), channel_id=1, source_target_pairs={{0,1},{1,0},{2,3},{3,2},{4,5},{5,4},{6,7},{7,6},{8,9},{9,8},{10,11... | collective-permute-start | bytes 1376264 | tf_op jit(solution)/shard_map/ppermute | solution.py:20
  71.6 18.0 %collective-permute-start.10 = (bf16[256,2048]{0,1:T(8,128)(2,1)S(1)}, bf16[256,2048]{0,1:T(8,128)(2,1)S(1)}, u32[]{:S(2)}, u32[]{:S(2)}) collective-permute-start(bf16[256,2048]{0,1:T(8,128)(2,1)S(1)} %broadcast_select_fusion), channel_id=1, source_target_pairs={{0,4},{4,0},{8,12},{12,8},{16,20},{20,16},{24,28},{28,24},{1,5},{5... | collective-permute-start | bytes 3145736 | tf_op jit(solution)/shard_map/ppermute | solution.py:20
  82.2 53.1 %collective-permute-start.8 = (bf16[256,2048]{0,1:T(8,128)(2,1)}, bf16[256,2048]{0,1:T(8,128)(2,1)}, u32[]{:S(2)}, u32[]{:S(2)}) collective-permute-start(bf16[256,2048]{0,1:T(8,128)(2,1)} %collective-permute-done.2), channel_id=1, source_target_pairs={{0,8},{4,12},{8,16},{12,20},{16,24},{20,28},{1,9},{5,13},{9,17},{1... | collective-permute-start | bytes 3145736 | tf_op jit(solution)/shard_map/ppermute | solution.py:160
  87.1 48.3 %collective-permute-start.9 = (bf16[256,2048]{0,1:T(8,128)(2,1)S(1)}, bf16[256,2048]{0,1:T(8,128)(2,1)}, u32[]{:S(2)}, u32[]{:S(2)}) collective-permute-start(bf16[256,2048]{0,1:T(8,128)(2,1)S(1)} %collective-permute-done.3), channel_id=1, source_target_pairs={{8,0},{12,4},{16,8},{20,12},{24,16},{28,20},{9,1},{13,5},{17,9},{2... | collective-permute-start | bytes 3145736 | tf_op jit(solution)/shard_map/ppermute | solution.py:161
  100.2 35.2 %collective-permute-start.11 = (bf16[2,64,1792]{2,1,0:T(8,128)(2,1)S(1)}, bf16[2,64,1792]{2,1,0:T(8,128)(2,1)}, u32[]{:S(2)}, u32[]{:S(2)}) collective-permute-start(bf16[2,64,1792]{2,1,0:T(8,128)(2,1)S(1)} %dynamic-slice_bitcast_fusion.13), channel_id=1, source_target_pairs={{0,1},{1,0},{2,3},{3,2},{4,5},{5,4},{6,7},{7,6},{8,9},{9,8},{10,11... | collective-permute-start | bytes 1376264 | tf_op jit(solution)/shard_map/ppermute | solution.py:20
  121.1 13.5 %collective-permute-start.24 = (bf16[2,64,1792]{2,1,0:T(8,128)(2,1)S(1)}, bf16[2,64,1792]{2,1,0:T(8,128)(2,1)S(1)}, u32[]{:S(2)}, u32[]{:S(2)}) collective-permute-start(bf16[2,64,1792]{2,1,0:T(8,128)(2,1)S(1)} %dynamic-slice_bitcast_fusion.6), channel_id=1, source_target_pairs={{0,2},{1,3},{2,0},{3,1},{4,6},{5,7},{6,4},{7,5},{8,10},{9,11},{10,... | collective-permute-start | bytes 1376264 | tf_op jit(solution)/shard_map/ppermute | solution.py:20
  122.7 17.7 %collective-permute-start.12 = (bf16[2,64,1792]{2,1,0:T(8,128)(2,1)S(1)}, bf16[2,64,1792]{2,1,0:T(8,128)(2,1)S(1)}, u32[]{:S(2)}, u32[]{:S(2)}) collective-permute-start(bf16[2,64,1792]{2,1,0:T(8,128)(2,1)S(1)} %dynamic-slice_bitcast_fusion.12), channel_id=1, source_target_pairs={{0,2},{1,3},{2,0},{3,1},{4,6},{5,7},{6,4},{7,5},{8,10},{9,11},{10,... | collective-permute-start | bytes 1376264 | tf_op jit(solution)/shard_map/ppermute | solution.py:20
  134.6 12.2 %collective-permute-start.22 = (bf16[2,64,1792]{2,1,0:T(8,128)(2,1)S(1)}, bf16[2,64,1792]{2,1,0:T(8,128)(2,1)S(1)}, u32[]{:S(2)}, u32[]{:S(2)}) collective-permute-start(bf16[2,64,1792]{2,1,0:T(8,128)(2,1)S(1)} %dynamic-slice_bitcast_fusion.7), channel_id=1, source_target_pairs={{0,1},{1,0},{2,3},{3,2},{4,5},{5,4},{6,7},{7,6},{8,9},{9,8},{10,11... | collective-permute-start | bytes 1376264 | tf_op jit(solution)/shard_map/ppermute | solution.py:20
  140.6 17.2 %collective-permute-start.25 = (bf16[64,3584]{1,0:T(8,128)(2,1)S(1)}, bf16[64,3584]{1,0:T(8,128)(2,1)S(1)}, u32[]{:S(2)}, u32[]{:S(2)}) collective-permute-start(bf16[64,3584]{1,0:T(8,128)(2,1)S(1)} %pad_maximum_fusion.14), channel_id=1, source_target_pairs={{0,1},{1,0},{2,3},{3,2},{4,5},{5,4},{6,7},{7,6},{8,9},{9,8},{10,11... | collective-permute-start | bytes 1376264 | tf_op jit(solution)/shard_map/ppermute | solution.py:20
  148.7 14.2 %collective-permute-start.19 = (bf16[256,2048]{0,1:T(8,128)(2,1)S(1)}, bf16[256,2048]{0,1:T(8,128)(2,1)S(1)}, u32[]{:S(2)}, u32[]{:S(2)}) collective-permute-start(bf16[256,2048]{0,1:T(8,128)(2,1)S(1)} %fusion.3), channel_id=1, source_target_pairs={{0,4},{4,0},{8,12},{12,8},{16,20},{20,16},{24,28},{28,24},{1,5},{5... | collective-permute-start | bytes 3145736 | tf_op jit(solution)/shard_map/ppermute | solution.py:20
  148.8 13.0 %collective-permute-start.23 = (bf16[64,3584]{1,0:T(8,128)(2,1)S(1)}, bf16[64,3584]{1,0:T(8,128)(2,1)S(1)}, u32[]{:S(2)}, u32[]{:S(2)}) collective-permute-start(bf16[64,3584]{1,0:T(8,128)(2,1)S(1)} %pad_maximum_fusion.13), channel_id=1, source_target_pairs={{0,2},{1,3},{2,0},{3,1},{4,6},{5,7},{6,4},{7,5},{8,10},{9,11},{10,... | collective-permute-start | bytes 1376264 | tf_op jit(solution)/shard_map/ppermute | solution.py:20
  150.4 60.1 %collective-permute-start.17 = (bf16[256,2048]{0,1:T(8,128)(2,1)}, bf16[256,2048]{0,1:T(8,128)(2,1)}, u32[]{:S(2)}, u32[]{:S(2)}) collective-permute-start(bf16[256,2048]{0,1:T(8,128)(2,1)} %collective-permute-done.8), channel_id=1, source_target_pairs={{0,8},{4,12},{8,16},{12,20},{16,24},{20,28},{1,9},{5,13},{9,17},{1... | collective-permute-start | bytes 3145736 | tf_op jit(solution)/shard_map/ppermute | solution.py:160
  155.1 55.4 %collective-permute-start.18 = (bf16[256,2048]{0,1:T(8,128)(2,1)}, bf16[256,2048]{0,1:T(8,128)(2,1)}, u32[]{:S(2)}, u32[]{:S(2)}) collective-permute-start(bf16[256,2048]{0,1:T(8,128)(2,1)} %collective-permute-done.9), channel_id=1, source_target_pairs={{8,0},{12,4},{16,8},{20,12},{24,16},{28,20},{9,1},{13,5},{17,9},{2... | collective-permute-start | bytes 3145736 | tf_op jit(solution)/shard_map/ppermute | solution.py:161
  179.9 30.6 %collective-permute-start.20 = (bf16[2,64,1792]{2,1,0:T(8,128)(2,1)S(1)}, bf16[2,64,1792]{2,1,0:T(8,128)(2,1)S(1)}, u32[]{:S(2)}, u32[]{:S(2)}) collective-permute-start(bf16[2,64,1792]{2,1,0:T(8,128)(2,1)S(1)} %dynamic-slice_bitcast_fusion.9), channel_id=1, source_target_pairs={{0,1},{1,0},{2,3},{3,2},{4,5},{5,4},{6,7},{7,6},{8,9},{9,8},{10,11... | collective-permute-start | bytes 1376264 | tf_op jit(solution)/shard_map/ppermute | solution.py:20
  195.4 13.5 %collective-permute-start.29 = (bf16[2,64,1792]{2,1,0:T(8,128)(2,1)S(1)}, bf16[2,64,1792]{2,1,0:T(8,128)(2,1)S(1)}, u32[]{:S(2)}, u32[]{:S(2)}) collective-permute-start(bf16[2,64,1792]{2,1,0:T(8,128)(2,1)S(1)} %dynamic-slice_bitcast_fusion.4), channel_id=1, source_target_pairs={{0,2},{1,3},{2,0},{3,1},{4,6},{5,7},{6,4},{7,5},{8,10},{9,11},{10,... | collective-permute-start | bytes 1376264 | tf_op jit(solution)/shard_map/ppermute | solution.py:20
  197.0 20.3 %collective-permute-start.21 = (bf16[2,64,1792]{2,1,0:T(8,128)(2,1)S(1)}, bf16[2,64,1792]{2,1,0:T(8,128)(2,1)S(1)}, u32[]{:S(2)}, u32[]{:S(2)}) collective-permute-start(bf16[2,64,1792]{2,1,0:T(8,128)(2,1)S(1)} %dynamic-slice_bitcast_fusion.8), channel_id=1, source_target_pairs={{0,2},{1,3},{2,0},{3,1},{4,6},{5,7},{6,4},{7,5},{8,10},{9,11},{10,... | collective-permute-start | bytes 1376264 | tf_op jit(solution)/shard_map/ppermute | solution.py:20
  220.9 13.5 %collective-permute-start.26 = (bf16[256,2048]{0,1:T(8,128)(2,1)S(1)}, bf16[256,2048]{0,1:T(8,128)(2,1)S(1)}, u32[]{:S(2)}, u32[]{:S(2)}) collective-permute-start(bf16[256,2048]{0,1:T(8,128)(2,1)S(1)} %select_select_fusion.1), channel_id=1, source_target_pairs={{0,4},{4,0},{8,12},{12,8},{16,20},{20,16},{24,28},{28,24},{1,5},{5... | collective-permute-start | bytes 3145736 | tf_op jit(solution)/shard_map/ppermute | solution.py:20
  221.0 13.0 %collective-permute-start.28 = (bf16[64,3584]{1,0:T(8,128)(2,1)S(1)}, bf16[64,3584]{1,0:T(8,128)(2,1)S(1)}, u32[]{:S(2)}, u32[]{:S(2)}) collective-permute-start(bf16[64,3584]{1,0:T(8,128)(2,1)S(1)} %pad_maximum_fusion.15), channel_id=1, source_target_pairs={{0,2},{1,3},{2,0},{3,1},{4,6},{5,7},{6,4},{7,5},{8,10},{9,11},{10,... | collective-permute-start | bytes 1376264 | tf_op jit(solution)/shard_map/ppermute | solution.py:20
  251.6 54.8 %collective-permute-start.39 = (bf16[2,64,1792]{2,1,0:T(8,128)(2,1)S(1)}, bf16[2,64,1792]{2,1,0:T(8,128)(2,1)S(1)}, u32[]{:S(2)}, u32[]{:S(2)}) collective-permute-start(bf16[2,64,1792]{2,1,0:T(8,128)(2,1)S(1)} %dynamic-slice_bitcast_fusion.3), channel_id=1, source_target_pairs={{0,1},{1,0},{2,3},{3,2},{4,5},{5,4},{6,7},{7,6},{8,9},{9,8},{10,11... | collective-permute-start | bytes 1376264 | tf_op jit(solution)/shard_map/ppermute | solution.py:20
  272.8 31.1 %collective-permute-start.42 = (bf16[2,64,1792]{2,1,0:T(8,128)(2,1)S(1)}, bf16[2,64,1792]{2,1,0:T(8,128)(2,1)S(1)}, u32[]{:S(2)}, u32[]{:S(2)}) collective-permute-start(bf16[2,64,1792]{2,1,0:T(8,128)(2,1)S(1)} %dynamic-slice_bitcast_fusion.1), channel_id=1, source_target_pairs={{0,2},{1,3},{2,0},{3,1},{4,6},{5,7},{6,4},{7,5},{8,10},{9,11},{10,... | collective-permute-start | bytes 1376264 | tf_op jit(solution)/shard_map/ppermute | solution.py:20
  274.9 30.0 %collective-permute-start.43 = (bf16[2,64,1792]{2,1,0:T(8,128)(2,1)S(1)}, bf16[2,64,1792]{2,1,0:T(8,128)(2,1)S(1)}, u32[]{:S(2)}, u32[]{:S(2)}) collective-permute-start(bf16[2,64,1792]{2,1,0:T(8,128)(2,1)S(1)} %dynamic-slice_bitcast_fusion), channel_id=1, source_target_pairs={{0,2},{1,3},{2,0},{3,1},{4,6},{5,7},{6,4},{7,5},{8,10},{9,11},{10,... | collective-permute-start | bytes 1376264 | tf_op jit(solution)/shard_map/ppermute | solution.py:20
  279.5 27.1 %collective-permute-start.40 = (bf16[2,64,1792]{2,1,0:T(8,128)(2,1)S(1)}, bf16[2,64,1792]{2,1,0:T(8,128)(2,1)S(1)}, u32[]{:S(2)}, u32[]{:S(2)}) collective-permute-start(bf16[2,64,1792]{2,1,0:T(8,128)(2,1)S(1)} %dynamic-slice_bitcast_fusion.2), channel_id=1, source_target_pairs={{0,1},{1,0},{2,3},{3,2},{4,5},{5,4},{6,7},{7,6},{8,9},{9,8},{10,11... | collective-permute-start | bytes 1376264 | tf_op jit(solution)/shard_map/ppermute | solution.py:20
  280.7 13.6 %collective-permute-start.38 = (bf16[2,64,896]{2,1,0:T(8,128)(2,1)S(1)}, bf16[2,64,896]{2,1,0:T(8,128)(2,1)S(1)}, u32[]{:S(2)}, u32[]{:S(2)}) collective-permute-start(bf16[2,64,896]{2,1,0:T(8,128)(2,1)S(1)} %pad_maximum_fusion.26), channel_id=1, source_target_pairs={{0,1},{1,0},{2,3},{3,2},{4,5},{5,4},{6,7},{7,6},{8,9},{9,8},{10,11... | collective-permute-start | bytes 688136 | tf_op jit(solution)/shard_map/ppermute | solution.py:20
  302.8 13.5 %collective-permute-start.32 = (bf16[2,64,1792]{2,1,0:T(8,128)(2,1)S(1)}, bf16[2,64,1792]{2,1,0:T(8,128)(2,1)S(1)}, u32[]{:S(2)}, u32[]{:S(2)}) collective-permute-start(bf16[2,64,1792]{2,1,0:T(8,128)(2,1)S(1)} %pad_maximum_fusion.17), channel_id=1, source_target_pairs={{0,2},{1,3},{2,0},{3,1},{4,6},{5,7},{6,4},{7,5},{8,10},{9,11},{10,... | collective-permute-start | bytes 1376264 | tf_op jit(solution)/shard_map/ppermute | solution.py:20
  303.9 13.5 %collective-permute-start.34 = (bf16[2,64,1792]{2,1,0:T(8,128)(2,1)S(1)}, bf16[2,64,1792]{2,1,0:T(8,128)(2,1)S(1)}, u32[]{:S(2)}, u32[]{:S(2)}) collective-permute-start(bf16[2,64,1792]{2,1,0:T(8,128)(2,1)S(1)} %pad_maximum_fusion.18), channel_id=1, source_target_pairs={{0,1},{1,0},{2,3},{3,2},{4,5},{5,4},{6,7},{7,6},{8,9},{9,8},{10,11... | collective-permute-start | bytes 1376264 | tf_op jit(solution)/shard_map/ppermute | solution.py:20
  305.1 19.0 %collective-permute-start.44 = (bf16[64,3584]{1,0:T(8,128)(2,1)S(1)}, bf16[64,3584]{1,0:T(8,128)(2,1)S(1)}, u32[]{:S(2)}, u32[]{:S(2)}) collective-permute-start(bf16[64,3584]{1,0:T(8,128)(2,1)S(1)} %pad_maximum_fusion.22), channel_id=1, source_target_pairs={{0,1},{1,0},{2,3},{3,2},{4,5},{5,4},{6,7},{7,6},{8,9},{9,8},{10,11... | collective-permute-start | bytes 1376264 | tf_op jit(solution)/shard_map/ppermute | solution.py:20
  306.7 17.4 %collective-permute-start.41 = (bf16[64,3584]{1,0:T(8,128)(2,1)S(1)}, bf16[64,3584]{1,0:T(8,128)(2,1)S(1)}, u32[]{:S(2)}, u32[]{:S(2)}) collective-permute-start(bf16[64,3584]{1,0:T(8,128)(2,1)S(1)} %pad_maximum_fusion.21), channel_id=1, source_target_pairs={{0,2},{1,3},{2,0},{3,1},{4,6},{5,7},{6,4},{7,5},{8,10},{9,11},{10,... | collective-permute-start | bytes 1376264 | tf_op jit(solution)/shard_map/ppermute | solution.py:20
  (42 other events, 261.0 us)
where the time goes:
time: 366 us; the launch traced here: 365 us
  waiting for transfers between devices  130 us (36%)
  local copies, waits for them, and re-layouts  71.3 us (19%)
  starting transfers between devices  65.3 us (18%)
  Pallas kernels  60.4 us (17%)
  other arithmetic  36.7 us (10%)
    ppermute x43, waiting for transfers between devices, swap(): return lax.ppermute(value, axis, [(i, i ^ mask) for i in range(size)])  130 us
    unnamed x57, local copies, waits for them, and re-layouts  53.8 us
    pallas_call x8, Pallas kernels, rows_products(): pl.pallas_call(functools.partial(rows_kernel, transposed), grid=(width //...  48 us
    ppermute x43, starting transfers between devices, swap(): return lax.ppermute(value, axis, [(i, i ^ mask) for i in range(size)])  47.1 us
    ppermute x3, starting transfers between devices, pass_on(): came['left', distance] = lax.ppermute(left, 'seq', rightward)  14.2 us
    concatenate x1, other arithmetic, body(): jnp.concatenate(all_second, axis=0)  13.7 us
    pallas_call x1, Pallas kernels, scaled_product(): pl.pallas_call(functools.partial(product_kernel, scale), grid=(rows // ti...  12.4 us
  transfers between devices with their start and end apart: 49, of which 24 were waited for; matrix products, arithmetic and copies ran while one was open for 10% of the time, Pallas kernels for 12%

commit v1 on v0

--- a/solution.py
+++ b/solution.py
@@ -44,13 +44,15 @@
             came = swap(jnp.concatenate(sent, axis=-1), "tensor", size, 1 << bit)
             came = [came[..., k * width : (k + 1) * width] for k in range(len(held))]
         first = came[0] if first is None else first
-        held = [
-            lax.dynamic_index_in_dim(h, mine, place, False).astype(jnp.float32)
-            + c.astype(jnp.float32)
-            for h, c in zip(held, came)
-        ]
+        held = [lax.dynamic_index_in_dim(h, mine, place, False) for h in held]
         left.pop(place)
-    return held, first
+        if left:
+            held = add(held, came)
+    return held, came, first
+
+
+def add(held, came):
+    return [h.astype(jnp.float32) + c.astype(jnp.float32) for h, c in zip(held, came)]
 
 
 def gather_rows(block, order, size):
@@ -73,45 +75,56 @@
     return ("left" if chip > chips - 1 - chip else "right", step - both)
 
 
-def product_kernel(scale, left_ref, right_ref, out_ref):
-    out_ref[...] = jnp.dot(left_ref[...], right_ref[...], preferred_element_type=jnp.float32) * scale
-
-
-def scaled_product(left, right, scale):
-    rows, depth = left.shape
-    width = right.shape[1]
+def product_kernel(scale, places, n_left, *refs):
+    lefts, rights, out_ref, right = refs[:n_left], refs[n_left:-2], refs[-2], refs[-1]
+
+    @pl.when(pl.program_id(0) == 0)
+    def _():
+        for (row, column), ref in zip(places, rights):
+            right[row : row + ref.shape[0], column : column + ref.shape[1]] = ref[...]
+
+    left = jnp.concatenate([ref[...] for ref in lefts], axis=0)
+    out_ref[...] = scale * lax.dot_general(
+        left, right[...], (((0,), (0,)), ((), ())), preferred_element_type=jnp.float32
+    )
+
+
+def scaled_product(lefts, left_rows, rights, places, scale):
+    depth = left_rows * len(lefts)
+    rows = lefts[0].shape[1]
+    width = max(column + right.shape[1] for (_, column), right in zip(places, rights))
     tile = 256
     return pl.pallas_call(
-        functools.partial(product_kernel, scale),
+        functools.partial(product_kernel, scale, places, len(lefts)),
         grid=(rows // tile,),
-        in_specs=[
-            pl.BlockSpec((tile, depth), lambda i: (i, 0)),
-            pl.BlockSpec((depth, width), lambda i: (0, 0)),
-        ],
+        in_specs=[pl.BlockSpec((left_rows, tile), lambda i: (0, i))] * len(lefts)
+        + [pl.BlockSpec(right.shape, lambda i: (0, 0)) for right in rights],
         out_specs=pl.BlockSpec((tile, width), lambda i: (i, 0)),
         out_shape=jax.ShapeDtypeStruct((rows, width), jnp.float32),
-        compiler_params=pltpu.CompilerParams(vmem_limit_bytes=32 * 1024 * 1024),
+        scratch_shapes=[pltpu.VMEM((depth, width), jnp.bfloat16)],
+        compiler_params=pltpu.CompilerParams(vmem_limit_bytes=60 * 1024 * 1024),
         cost_estimate=pl.CostEstimate(
             flops=2 * rows * depth * width,
             bytes_accessed=2 * depth * (rows + width) + 4 * rows * width,
             transcendentals=0,
         ),
-    )(left, right)
-
-
-def rows_kernel(transposed, left_ref, *refs):
+    )(*lefts, *rights)
+
+
+def rows_kernel(transposed, upper_ref, lower_ref, *refs):
     weights, outs = refs[: len(refs) // 2], refs[len(refs) // 2 :]
+    left = jnp.concatenate([upper_ref[...], lower_ref[...]], axis=0)
     for weight_ref, out_ref in zip(weights, outs):
         out_ref[...] = lax.dot_general(
-            left_ref[...],
+            left,
             weight_ref[...],
             (((1,), (1 if transposed else 0,)), ((), ())),
             preferred_element_type=jnp.float32,
         ).astype(out_ref.dtype)
 
 
-def rows_products(left, weights, transposed):
-    rows, depth = left.shape
+def rows_products(upper, lower, part, half_rows, weights, transposed):
+    rows, depth = 2 * half_rows, upper.shape[1]
     width = weights[0].shape[0 if transposed else 1]
     tile = 256 if width % 256 == 0 else 128
     if transposed:
@@ -122,16 +135,16 @@
     return pl.pallas_call(
         functools.partial(rows_kernel, transposed),
         grid=(width // tile,),
-        in_specs=[pl.BlockSpec((rows, depth), lambda i: (0, 0))] + [weight_spec] * count,
+        in_specs=[pl.BlockSpec((half_rows, depth), lambda i: (part, 0))] * 2 + [weight_spec] * count,
         out_specs=[pl.BlockSpec((rows, tile), lambda i: (0, i))] * count,
         out_shape=[jax.ShapeDtypeStruct((rows, width), jnp.bfloat16)] * count,
-        compiler_params=pltpu.CompilerParams(vmem_limit_bytes=24 * 1024 * 1024),
+        compiler_params=pltpu.CompilerParams(vmem_limit_bytes=60 * 1024 * 1024),
         cost_estimate=pl.CostEstimate(
             flops=2 * count * rows * depth * width,
             bytes_accessed=2 * (rows * depth + count * width * (rows + depth)),
             transcendentals=0,
         ),
-    )(left, *weights)
+    )(upper, lower, *weights)
 
 
 def body(n_seq, n_tensor, tokens, cotangent, gain, w_gate, w_up, w_down, probe):
@@ -163,59 +176,64 @@
     pass_on(1, ())
     chip = lax.axis_index("seq") // 2
 
-    def products(norm_rows, cot_rows):
-        return [
-            *rows_products(cot_rows, [w_down], True),
-            *rows_products(norm_rows, [probe, w_gate, w_up], False),
-        ]
-
     def gathered(one, other):
         return [gather_rows(one, up_order, n_tensor), gather_rows(other, down_order, n_tensor)]
 
-    def gathered_alone(second):
+    all_norm, rights, places, firsts, seconds = [], [], [], [], []
+    unfinished = None
+
+    def finished(waited):
+        held, came = unfinished
+        upstream, pre_gate, tangent, pre_up = add(held, after(came, waited))
+        return second_factor(pre_gate, pre_up, tangent, upstream)
+
+    def gather_last(step, second):
         half = second.shape[1] // 2
-        return jnp.concatenate(gathered(second[:, :half], second[:, half:]), axis=1)
-
-    all_norm, all_second, firsts, seconds = [], [], [], []
+        rights.extend(gathered(second[:, :half], second[:, half:]))
+        places.extend([(2 * rows * step, 0), (2 * rows * step, half)])
+
     for step in range(chips):
         if step == 0:
-            cot_rows = jnp.concatenate([cotangent, swap(cotangent, "seq", n_seq, 1)], axis=0)
-            norm_rows = jnp.concatenate([normed, swap(normed, "seq", n_seq, 1)], axis=0)
+            cots = (cotangent, swap(cotangent, "seq", n_seq, 1), 0)
+            norms = (normed, swap(normed, "seq", n_seq, 1), 0)
         else:
             where_from = [arrival(c, step, chips) for c in range(chips)]
             kinds = sorted(set(where_from))
-            candidates = after([came[kind] for kind in kinds], (firsts[step - 1], seconds[: step - 1]))
+            candidates = after([came[kind] for kind in kinds], (firsts[step - 1], seconds))
             block = candidates[0]
             for kind, candidate in zip(kinds[1:], candidates[1:]):
                 for c in range(chips):
                     if where_from[c] == kind:
                         block = jnp.where(chip == c, candidate, block)
             other = swap(block, "seq", n_seq, 1)
-            norm_rows = jnp.concatenate([block[:rows], other[:rows]], axis=0)
-            cot_rows = jnp.concatenate([block[rows:], other[rows:]], axis=0)
-        all_norm.append(norm_rows)
+            cots = (block, other, 1)
+            norms = (block, other, 0)
+        all_norm += norms[:2]
+
+        parts = [
+            *rows_products(*cots, rows, [w_down], True),
+            *rows_products(*norms, rows, [probe, w_gate, w_up], False),
+        ]
+        if step > 0:
+            seconds.append(finished(parts))
         if step == chips - 1:
-            norm_columns = jnp.concatenate(all_norm, axis=0).T
-            cot_rows, norm_columns = lax.optimization_barrier((cot_rows, norm_columns))
-
-        parts = products(norm_rows, cot_rows)
-        if step == chips - 1:
-            ready = after(seconds, parts)
+            ready = list(enumerate(after(seconds, parts)))
             while len(ready) > 1:
-                all_second += gathered(ready[0], ready[1])
+                rights += gathered(ready[0][1], ready[1][1])
+                places += [(2 * rows * ready[0][0], 0), (2 * rows * ready[1][0], 0)]
                 ready = ready[2:]
-            all_second += [gathered_alone(one) for one in ready]
+            for index, second in ready:
+                gather_last(index, second)
         upstream, tangent, pre_gate, pre_up = parts
-        (upstream, pre_gate), first = scatter_sum([upstream, pre_gate], up_order, n_tensor)
-        (tangent, pre_up), other_first = scatter_sum([tangent, pre_up], down_order, n_tensor)
+        held, last, first = scatter_sum([upstream, pre_gate], up_order, n_tensor)
+        other_held, other_last, other_first = scatter_sum([tangent, pre_up], down_order, n_tensor)
+        unfinished = (held + other_held, last + other_last)
         firsts.append((first, other_first))
         if step < chips - 2:
             pass_on(step + 2, (firsts[-1], seconds))
-        second = second_factor(pre_gate, pre_up, tangent, upstream)
-        seconds.append(second)
-
-    all_second.append(gathered_alone(seconds[-1]))
-    return scaled_product(norm_columns, jnp.concatenate(all_second, axis=0), 1.0 / total_tokens)
+
+    gather_last(chips - 1, finished(()))
+    return scaled_product(all_norm, rows, rights, places, 1.0 / total_tokens)
 
 
 def solution(mesh):

time: 366 us -> 339 us (0.926)
  Pallas kernels: 60.4 us -> 101 us
  local copies, waits for them, and re-layouts: 71.3 us -> 37.1 us
  waiting for transfers between devices: 130 us -> 108 us
  other arithmetic: 36.7 us -> 28 us
    unnamed x57 -> x86, local copies, waits for them, and re-layouts: 53.8 us -> 9.15 us
    pallas_call x8, Pallas kernels: 48 us -> 86.3 us  [rows_products(): pl.pallas_call(functools.partial(rows_kernel, transposed), grid=(width //...]
    ppermute x43, waiting for transfers between devices: 130 us -> 108 us  [swap(): return lax.ppermute(value, axis, [(i, i ^ mask) for i in range(size)])]
    concatenate x8 -> x1, other arithmetic: 23.2 us -> 2.23 us  [body(): own = jnp.concatenate([normed, cotangent], axis=0)]
    squeeze x16, local copies, waits for them, and re-layouts: 1.35 us -> 20.5 us  [scatter_sum(): lax.dynamic_index_in_dim(h, 1 - mine, place, False).astype(jnp.bfloat16)]
    concatenate x6 -> x0, local copies, waits for them, and re-layouts: 10.8 us -> none  [the longest x3 6.43 us: body(): norm_rows = jnp.concatenate([block[:rows], other[:rows]], axis=0)]
    add x16, other arithmetic: 3.59 us -> 8.7 us  [add(): h.astype(jnp.float32) + c.astype(jnp.float32)]
  transfers between devices with their start and end apart: 49 -> 49, of which waited for: 24 -> 21; matrix products, arithmetic and copies ran while one was open for 10% -> 15% of each run, Pallas kernels for 12% -> 23%
where the time goes in v1:
time: 339 us; the launch traced here: 337 us
  waiting for transfers between devices  108 us (32%)
  Pallas kernels  101 us (30%)
  starting transfers between devices  61.9 us (18%)
  local copies, waits for them, and re-layouts  37.1 us (11%)
  other arithmetic  28 us (8%)
    ppermute x43, waiting for transfers between devices, swap(): return lax.ppermute(value, axis, [(i, i ^ mask) for i in range(size)])  108 us
    pallas_call x8, Pallas kernels, rows_products(): pl.pallas_call(functools.partial(rows_kernel, transposed), grid=(width //...  86.3 us
    ppermute x43, starting transfers between devices, swap(): return lax.ppermute(value, axis, [(i, i ^ mask) for i in range(size)])  44.2 us
    squeeze x16, local copies, waits for them, and re-layouts, scatter_sum(): lax.dynamic_index_in_dim(h, 1 - mine, place, False).astype(jnp.bfloat16)  20.5 us
    pallas_call x1, Pallas kernels, scaled_product(): pl.pallas_call(functools.partial(product_kernel, scale, places, len(lefts...  14.9 us
    ppermute x3, starting transfers between devices, pass_on(): came['left', distance] = lax.ppermute(left, 'seq', rightward)  13.7 us
    unnamed x86, local copies, waits for them, and re-layouts  9.15 us
    add x16, other arithmetic, add(): h.astype(jnp.float32) + c.astype(jnp.float32)  8.7 us
  transfers between devices with their start and end apart: 49, of which 21 were waited for; matrix products, arithmetic and copies ran while one was open for 15% of the time, Pallas kernels for 23%

profile of v1, /device:TPU:0, one launch (start us, length us, event | category | flops | bytes accessed | tf_op | source)
XLA Modules:
  0.0 336.8 jit_solution(13370119008288549304)
XLA Ops:
  1.2 3.0 collective-permute-start
  5.7 2.0 collective-permute-start.1
  10.7 2.2 pad_maximum_fusion
  12.9 4.1 %collective-permute-start.3 = (bf16[256,2048]{1,0:T(8,128)(2,1)}, bf16[256,2048]{1,0:T(8,128)(2,1)S(1)}, u32[]{:S(2)}, u32[]{:S(2)}) collective-permute-start(bf16[256,2048]{1,0:T(8,128)(2,1)} %pad_maximum_fusion), channel_id=1, source_target_pairs={{0,8},{4,12},{8,16},{12,20},{16,24},{20,28},{1,9},{5,13},{9,17},{1... | collective-permute-start | bytes 3145736 | tf_op jit(solution)/shard_map/ppermute | solution.py:173
  19.1 8.0 %shard_map.73 = bf16[256,1792]{1,0:T(8,128)(2,1)} custom-call(bf16[128,2048]{1,0:T(8,128)(2,1)} %upper_ref.1, bf16[128,2048]{1,0:T(8,128)(2,1)} %copy-done.42, bf16[1792,2048]{1,0:T(8,128)(2,1)} %refs_0_.14), custom_call_target="tpu_custom_call" | custom-call | flops 1879048192 | bytes 9306112 | tf_op jit(solution)/shard_map/pallas_call | solution.py:135
  30.4 13.6 %shard_map.74 = (bf16[256,1792]{1,0:T(8,128)(2,1)}, bf16[256,1792]{1,0:T(8,128)(2,1)}, bf16[256,1792]{1,0:T(8,128)(2,1)}) custom-call(bf16[128,2048]{1,0:T(8,128)(2,1)} %copy-done.3, bf16[128,2048]{1,0:T(8,128)(2,1)} %collective-permute-done.2.lower_ref.refs_1_, bf16[2048,1792]{1,0:T(8,128)(2,1)} %refs_0_.15, bf16[2048,1792]{1,0:T(8,128)(2,1)} %refs_1_.7, ...), custom_call_target="tpu_custom_call" | custom-call | flops 5637144576 | bytes 25821184 | tf_op jit(solution)/shard_map/pallas_call | solution.py:135
  51.2 7.4 %collective-permute-done.15 = bf16[2,64,1792]{2,1,0:T(8,128)(2,1)S(1)} collective-permute-done((bf16[2,64,1792]{2,1,0:T(8,128)(2,1)S(1)}, bf16[2,64,1792]{2,1,0:T(8,128)(2,1)S(1)}, u32[]{:S(2)}, u32[]{:S(2)}) %collective-permute-start.15) | collective-permute-done | bytes 458784 | tf_op jit(solution)/shard_map/ppermute | solution.py:20
  59.8 7.5 %collective-permute-done.7 = bf16[2,64,1792]{2,1,0:T(8,128)(2,1)S(1)} collective-permute-done((bf16[2,64,1792]{2,1,0:T(8,128)(2,1)S(1)}, bf16[2,64,1792]{2,1,0:T(8,128)(2,1)S(1)}, u32[]{:S(2)}, u32[]{:S(2)}) %collective-permute-start.7) | collective-permute-done | bytes 458784 | tf_op jit(solution)/shard_map/ppermute | solution.py:20
  73.3 5.9 %collective-permute-start.9 = (bf16[256,2048]{1,0:T(8,128)(2,1)}, bf16[256,2048]{1,0:T(8,128)(2,1)}, u32[]{:S(2)}, u32[]{:S(2)}) collective-permute-start(bf16[256,2048]{1,0:T(8,128)(2,1)} %copy-done.26), channel_id=1, source_target_pairs={{0,8},{4,12},{8,16},{12,20},{16,24},{20,28},{1,9},{5,13},{9,17},{1... | collective-permute-start | bytes 3145736 | tf_op jit(solution)/shard_map/ppermute | solution.py:173
  80.0 3.4 %collective-permute-done.14 = bf16[64,3584]{1,0:T(8,128)(2,1)S(1)} collective-permute-done((bf16[64,3584]{1,0:T(8,128)(2,1)S(1)}, bf16[64,3584]{1,0:T(8,128)(2,1)S(1)}, u32[]{:S(2)}, u32[]{:S(2)}) %collective-permute-start.14) | collective-permute-done | bytes 458784 | tf_op jit(solution)/shard_map/ppermute | solution.py:20
  85.2 8.0 %shard_map.75 = bf16[256,1792]{1,0:T(8,128)(2,1)} custom-call(bf16[256,2048]{1,0:T(8,128)(2,1)} %copy-done.1, bf16[256,2048]{1,0:T(8,128)(2,1)} %copy-done.4, bf16[1792,2048]{1,0:T(8,128)(2,1)} %refs_0_.14), custom_call_target="tpu_custom_call" | custom-call | flops 1879048192 | bytes 9306112 | tf_op jit(solution)/shard_map/pallas_call | solution.py:135
  96.5 13.6 %shard_map.76 = (bf16[256,1792]{1,0:T(8,128)(2,1)}, bf16[256,1792]{1,0:T(8,128)(2,1)}, bf16[256,1792]{1,0:T(8,128)(2,1)}) custom-call(bf16[256,2048]{1,0:T(8,128)(2,1)} %copy-done.1, bf16[256,2048]{1,0:T(8,128)(2,1)} %copy-done.4, bf16[2048,1792]{1,0:T(8,128)(2,1)} %refs_0_.15, bf16[2048,1792]{1,0:T(8,128)(2,1)} %refs_1_.7, bf16[2048,1792]{1,0:T(8,128)(2,1)} %refs_2_.7), custom_call_target="tpu_custom_call" | custom-call | flops 5637144576 | bytes 25821184 | tf_op jit(solution)/shard_map/pallas_call | solution.py:135
  114.6 2.4 fusion.7
  118.0 8.0 %collective-permute-done.24 = bf16[2,64,1792]{2,1,0:T(8,128)(2,1)S(1)} collective-permute-done((bf16[2,64,1792]{2,1,0:T(8,128)(2,1)S(1)}, bf16[2,64,1792]{2,1,0:T(8,128)(2,1)S(1)}, u32[]{:S(2)}, u32[]{:S(2)}) %collective-permute-start.24) | collective-permute-done | bytes 458784 | tf_op jit(solution)/shard_map/ppermute | solution.py:20
  127.7 6.6 %collective-permute-done.12 = bf16[2,64,1792]{2,1,0:T(8,128)(2,1)S(1)} collective-permute-done((bf16[2,64,1792]{2,1,0:T(8,128)(2,1)S(1)}, bf16[2,64,1792]{2,1,0:T(8,128)(2,1)S(1)}, u32[]{:S(2)}, u32[]{:S(2)}) %collective-permute-start.12) | collective-permute-done | bytes 458784 | tf_op jit(solution)/shard_map/ppermute | solution.py:20
  141.8 3.7 %collective-permute-start.18 = (bf16[256,2048]{1,0:T(8,128)(2,1)}, bf16[256,2048]{1,0:T(8,128)(2,1)}, u32[]{:S(2)}, u32[]{:S(2)}) collective-permute-start(bf16[256,2048]{1,0:T(8,128)(2,1)} %collective-permute-done.9), channel_id=1, source_target_pairs={{0,8},{4,12},{8,16},{12,20},{16,24},{20,28},{1,9},{5,13},{9,17},{1... | collective-permute-start | bytes 3145736 | tf_op jit(solution)/shard_map/ppermute | solution.py:173
  147.8 5.4 %collective-permute-done.23 = bf16[64,3584]{1,0:T(8,128)(2,1)S(1)} collective-permute-done((bf16[64,3584]{1,0:T(8,128)(2,1)S(1)}, bf16[64,3584]{1,0:T(8,128)(2,1)S(1)}, u32[]{:S(2)}, u32[]{:S(2)}) %collective-permute-start.23) | collective-permute-done | bytes 458784 | tf_op jit(solution)/shard_map/ppermute | solution.py:20
  155.0 8.1 %shard_map.77 = bf16[256,1792]{1,0:T(8,128)(2,1)} custom-call(bf16[256,2048]{1,0:T(8,128)(2,1)} %copy-done, bf16[256,2048]{1,0:T(8,128)(2,1)} %copy-done.5, bf16[1792,2048]{1,0:T(8,128)(2,1)} %refs_0_.14), custom_call_target="tpu_custom_call" | custom-call | flops 1879048192 | bytes 9306112 | tf_op jit(solution)/shard_map/pallas_call | solution.py:135
  166.3 13.5 %shard_map.78 = (bf16[256,1792]{1,0:T(8,128)(2,1)}, bf16[256,1792]{1,0:T(8,128)(2,1)}, bf16[256,1792]{1,0:T(8,128)(2,1)}) custom-call(bf16[256,2048]{1,0:T(8,128)(2,1)} %copy-done, bf16[256,2048]{1,0:T(8,128)(2,1)} %copy-done.5, bf16[2048,1792]{1,0:T(8,128)(2,1)} %refs_0_.15, bf16[2048,1792]{1,0:T(8,128)(2,1)} %refs_1_.7, bf16[2048,1792]{1,0:T(8,128)(2,1)} %refs_2_.7), custom_call_target="tpu_custom_call" | custom-call | flops 5637144576 | bytes 25821184 | tf_op jit(solution)/shard_map/pallas_call | solution.py:135
  184.2 2.2 fusion.11
  187.4 8.2 %collective-permute-done.29 = bf16[2,64,1792]{2,1,0:T(8,128)(2,1)S(1)} collective-permute-done((bf16[2,64,1792]{2,1,0:T(8,128)(2,1)S(1)}, bf16[2,64,1792]{2,1,0:T(8,128)(2,1)S(1)}, u32[]{:S(2)}, u32[]{:S(2)}) %collective-permute-start.29) | collective-permute-done | bytes 458784 | tf_op jit(solution)/shard_map/ppermute | solution.py:20
  197.5 6.5 %collective-permute-done.21 = bf16[2,64,1792]{2,1,0:T(8,128)(2,1)S(1)} collective-permute-done((bf16[2,64,1792]{2,1,0:T(8,128)(2,1)S(1)}, bf16[2,64,1792]{2,1,0:T(8,128)(2,1)S(1)}, u32[]{:S(2)}, u32[]{:S(2)}) %collective-permute-start.21) | collective-permute-done | bytes 458784 | tf_op jit(solution)/shard_map/ppermute | solution.py:20
  211.5 3.7 %collective-permute-done.30 = bf16[64,3584]{1,0:T(8,128)(2,1)S(1)} collective-permute-done((bf16[64,3584]{1,0:T(8,128)(2,1)S(1)}, bf16[64,3584]{1,0:T(8,128)(2,1)S(1)}, u32[]{:S(2)}, u32[]{:S(2)}) %collective-permute-start.30) | collective-permute-done | bytes 458784 | tf_op jit(solution)/shard_map/ppermute | solution.py:20
  216.0 6.9 %collective-permute-done.28 = bf16[64,3584]{1,0:T(8,128)(2,1)S(1)} collective-permute-done((bf16[64,3584]{1,0:T(8,128)(2,1)S(1)}, bf16[64,3584]{1,0:T(8,128)(2,1)S(1)}, u32[]{:S(2)}, u32[]{:S(2)}) %collective-permute-start.28) | collective-permute-done | bytes 458784 | tf_op jit(solution)/shard_map/ppermute | solution.py:20
  224.7 8.0 %shard_map.79 = bf16[256,1792]{1,0:T(8,128)(2,1)} custom-call(bf16[256,2048]{1,0:T(8,128)(2,1)} %copy-done.2, bf16[256,2048]{1,0:T(8,128)(2,1)} %copy-done.6, bf16[1792,2048]{1,0:T(8,128)(2,1)} %refs_0_.14), custom_call_target="tpu_custom_call" | custom-call | flops 1879048192 | bytes 9306112 | tf_op jit(solution)/shard_map/pallas_call | solution.py:135
  235.8 13.5 %shard_map.80 = (bf16[256,1792]{1,0:T(8,128)(2,1)}, bf16[256,1792]{1,0:T(8,128)(2,1)}, bf16[256,1792]{1,0:T(8,128)(2,1)}) custom-call(bf16[256,2048]{1,0:T(8,128)(2,1)} %copy-done.2, bf16[256,2048]{1,0:T(8,128)(2,1)} %copy-done.6, bf16[2048,1792]{1,0:T(8,128)(2,1)} %refs_0_.15, bf16[2048,1792]{1,0:T(8,128)(2,1)} %refs_1_.7, bf16[2048,1792]{1,0:T(8,128)(2,1)} %refs_2_.7), custom_call_target="tpu_custom_call" | custom-call | flops 5637144576 | bytes 25821184 | tf_op jit(solution)/shard_map/pallas_call | solution.py:135
  264.7 10.9 %collective-permute-done.36 = bf16[2,64,896]{2,1,0:T(8,128)(2,1)S(1)} collective-permute-done((bf16[2,64,896]{2,1,0:T(8,128)(2,1)S(1)}, bf16[2,64,896]{2,1,0:T(8,128)(2,1)S(1)}, u32[]{:S(2)}, u32[]{:S(2)}) %collective-permute-start.36) | collective-permute-done | bytes 229408 | tf_op jit(solution)/shard_map/ppermute | solution.py:20
  283.3 5.8 %collective-permute-done.43 = bf16[2,64,1792]{2,1,0:T(8,128)(2,1)S(1)} collective-permute-done((bf16[2,64,1792]{2,1,0:T(8,128)(2,1)S(1)}, bf16[2,64,1792]{2,1,0:T(8,128)(2,1)S(1)}, u32[]{:S(2)}, u32[]{:S(2)}) %collective-permute-start.43) | collective-permute-done | bytes 458784 | tf_op jit(solution)/shard_map/ppermute | solution.py:20
  290.2 8.7 %collective-permute-done.32 = bf16[2,64,1792]{2,1,0:T(8,128)(2,1)S(1)} collective-permute-done((bf16[2,64,1792]{2,1,0:T(8,128)(2,1)S(1)}, bf16[2,64,1792]{2,1,0:T(8,128)(2,1)S(1)}, u32[]{:S(2)}, u32[]{:S(2)}) %collective-permute-start.32) | collective-permute-done | bytes 458784 | tf_op jit(solution)/shard_map/ppermute | solution.py:20
  299.0 7.2 %collective-permute-done.41 = bf16[64,3584]{1,0:T(8,128)(2,1)S(1)} collective-permute-done((bf16[64,3584]{1,0:T(8,128)(2,1)S(1)}, bf16[64,3584]{1,0:T(8,128)(2,1)S(1)}, u32[]{:S(2)}, u32[]{:S(2)}) %collective-permute-start.41) | collective-permute-done | bytes 458784 | tf_op jit(solution)/shard_map/ppermute | solution.py:20
  315.9 3.4 %collective-permute-done.46 = bf16[2,64,896]{2,1,0:T(8,128)(2,1)S(1)} collective-permute-done((bf16[2,64,896]{2,1,0:T(8,128)(2,1)S(1)}, bf16[2,64,896]{2,1,0:T(8,128)(2,1)S(1)}, u32[]{:S(2)}, u32[]{:S(2)}) %collective-permute-start.46) | collective-permute-done | bytes 229408 | tf_op jit(solution)/shard_map/ppermute | solution.py:20
  321.9 14.9 %shard_map.81 = f32[2048,1792]{1,0:T(8,128)} custom-call(bf16[128,2048]{1,0:T(8,128)(2,1)} %copy-done.3, bf16[128,2048]{1,0:T(8,128)(2,1)} %collective-permute-done.2.lower_ref.refs_1_, bf16[256,2048]{1,0:T(8,128)(2,1)} %copy-done.1, bf16[256,2048]{1,0:T(8,128)(2,1)} %copy-done.4, bf16[256,2048]{1,0:T(8,128)(2,1)} %copy-done, bf16[256,2048]{1,0:T(8,128)(2,1)} %copy-done.5, ...), custom_call_target="tpu_custom_call" | custom-call | flops 7516192768 | bytes 22544384 | tf_op jit(solution)/shard_map/pallas_call | solution.py:97
  (262 shorter events, 109.8 us)
Async XLA Ops:
  4.2 14.0 %collective-permute-start.5 = (bf16[128,2048]{1,0:T(8,128)(2,1)}, bf16[128,2048]{1,0:T(8,128)(2,1)S(1)}, u32[]{:S(2)}, u32[]{:S(2)}) collective-permute-start(bf16[128,2048]{1,0:T(8,128)(2,1)} %upper_ref.1), channel_id=1, source_target_pairs={{0,4},{4,0},{8,12},{12,8},{16,20},{20,16},{24,28},{28,24},{1,5},{5... | collective-permute-start | bytes 1572872 | tf_op jit(solution)/shard_map/ppermute | solution.py:20
  10.6 19.9 %collective-permute-start.2 = (bf16[128,2048]{1,0:T(8,128)(2,1)S(1)}, bf16[128,2048]{1,0:T(8,128)(2,1)}, u32[]{:S(2)}, u32[]{:S(2)}) collective-permute-start(bf16[128,2048]{1,0:T(8,128)(2,1)S(1)} %fusion.2.upper_ref.refs_0_), channel_id=1, source_target_pairs={{0,4},{4,0},{8,12},{12,8},{16,20},{20,16},{24,28},{28,24},{1,5},{5... | collective-permute-start | bytes 1572872 | tf_op jit(solution)/shard_map/ppermute | solution.py:20
  12.9 55.4 %collective-permute-start.3 = (bf16[256,2048]{1,0:T(8,128)(2,1)}, bf16[256,2048]{1,0:T(8,128)(2,1)S(1)}, u32[]{:S(2)}, u32[]{:S(2)}) collective-permute-start(bf16[256,2048]{1,0:T(8,128)(2,1)} %pad_maximum_fusion), channel_id=1, source_target_pairs={{0,8},{4,12},{8,16},{12,20},{16,24},{20,28},{1,9},{5,13},{9,17},{1... | collective-permute-start | bytes 3145736 | tf_op jit(solution)/shard_map/ppermute | solution.py:173
  17.0 52.3 %collective-permute-start.4 = (bf16[256,2048]{1,0:T(8,128)(2,1)}, bf16[256,2048]{1,0:T(8,128)(2,1)S(1)}, u32[]{:S(2)}, u32[]{:S(2)}) collective-permute-start(bf16[256,2048]{1,0:T(8,128)(2,1)} %pad_maximum_fusion), channel_id=1, source_target_pairs={{8,0},{12,4},{16,8},{20,12},{24,16},{28,20},{9,1},{13,5},{17,9},{2... | collective-permute-start | bytes 3145736 | tf_op jit(solution)/shard_map/ppermute | solution.py:174
  28.9 20.5 %collective-permute-start.6 = (bf16[2,64,1792]{2,1,0:T(8,128)(2,1)}, bf16[2,64,1792]{2,1,0:T(8,128)(2,1)}, u32[]{:S(2)}, u32[]{:S(2)}) collective-permute-start(bf16[2,64,1792]{2,1,0:T(8,128)(2,1)} %dynamic-slice_bitcast_fusion.15), channel_id=1, source_target_pairs={{0,1},{1,0},{2,3},{3,2},{4,5},{5,4},{6,7},{7,6},{8,9},{9,8},{10,11... | collective-permute-start | bytes 1376264 | tf_op jit(solution)/shard_map/ppermute | solution.py:20
  45.2 13.5 %collective-permute-start.15 = (bf16[2,64,1792]{2,1,0:T(8,128)(2,1)S(1)}, bf16[2,64,1792]{2,1,0:T(8,128)(2,1)S(1)}, u32[]{:S(2)}, u32[]{:S(2)}) collective-permute-start(bf16[2,64,1792]{2,1,0:T(8,128)(2,1)S(1)} %dynamic-slice_bitcast_fusion.10), channel_id=1, source_target_pairs={{0,2},{1,3},{2,0},{3,1},{4,6},{5,7},{6,4},{7,5},{8,10},{9,11},{10,... | collective-permute-start | bytes 1376264 | tf_op jit(solution)/shard_map/ppermute | solution.py:20
  47.8 19.5 %collective-permute-start.7 = (bf16[2,64,1792]{2,1,0:T(8,128)(2,1)S(1)}, bf16[2,64,1792]{2,1,0:T(8,128)(2,1)S(1)}, u32[]{:S(2)}, u32[]{:S(2)}) collective-permute-start(bf16[2,64,1792]{2,1,0:T(8,128)(2,1)S(1)} %dynamic-slice_bitcast_fusion.14), channel_id=1, source_target_pairs={{0,2},{1,3},{2,0},{3,1},{4,6},{5,7},{6,4},{7,5},{8,10},{9,11},{10,... | collective-permute-start | bytes 1376264 | tf_op jit(solution)/shard_map/ppermute | solution.py:20
  49.5 18.7 %collective-permute-start.13 = (bf16[2,64,1792]{2,1,0:T(8,128)(2,1)S(1)}, bf16[2,64,1792]{2,1,0:T(8,128)(2,1)S(1)}, u32[]{:S(2)}, u32[]{:S(2)}) collective-permute-start(bf16[2,64,1792]{2,1,0:T(8,128)(2,1)S(1)} %dynamic-slice_bitcast_fusion.11), channel_id=1, source_target_pairs={{0,1},{1,0},{2,3},{3,2},{4,5},{5,4},{6,7},{7,6},{8,9},{9,8},{10,11... | collective-permute-start | bytes 1376264 | tf_op jit(solution)/shard_map/ppermute | solution.py:20
  70.3 13.9 %collective-permute-start.8 = (bf16[256,2048]{1,0:T(8,128)(2,1)S(1)}, bf16[256,2048]{1,0:T(8,128)(2,1)S(1)}, u32[]{:S(2)}, u32[]{:S(2)}) collective-permute-start(bf16[256,2048]{1,0:T(8,128)(2,1)S(1)} %broadcast_select_fusion.upper_ref.refs_2_), channel_id=1, source_target_pairs={{0,4},{4,0},{8,12},{12,8},{16,20},{20,16},{24,28},{28,24},{1,5},{5... | collective-permute-start | bytes 3145736 | tf_op jit(solution)/shard_map/ppermute | solution.py:20
  70.4 13.0 %collective-permute-start.14 = (bf16[64,3584]{1,0:T(8,128)(2,1)S(1)}, bf16[64,3584]{1,0:T(8,128)(2,1)S(1)}, u32[]{:S(2)}, u32[]{:S(2)}) collective-permute-start(bf16[64,3584]{1,0:T(8,128)(2,1)S(1)} %pad_maximum_fusion.3), channel_id=1, source_target_pairs={{0,2},{1,3},{2,0},{3,1},{4,6},{5,7},{6,4},{7,5},{8,10},{9,11},{10,... | collective-permute-start | bytes 1376264 | tf_op jit(solution)/shard_map/ppermute | solution.py:20
  72.0 55.7 %collective-permute-start.10 = (bf16[256,2048]{1,0:T(8,128)(2,1)S(1)}, bf16[256,2048]{1,0:T(8,128)(2,1)}, u32[]{:S(2)}, u32[]{:S(2)}) collective-permute-start(bf16[256,2048]{1,0:T(8,128)(2,1)S(1)} %collective-permute-done.4), channel_id=1, source_target_pairs={{8,0},{12,4},{16,8},{20,12},{24,16},{28,20},{9,1},{13,5},{17,9},{2... | collective-permute-start | bytes 3145736 | tf_op jit(solution)/shard_map/ppermute | solution.py:174
  73.3 54.4 %collective-permute-start.9 = (bf16[256,2048]{1,0:T(8,128)(2,1)}, bf16[256,2048]{1,0:T(8,128)(2,1)}, u32[]{:S(2)}, u32[]{:S(2)}) collective-permute-start(bf16[256,2048]{1,0:T(8,128)(2,1)} %copy-done.26), channel_id=1, source_target_pairs={{0,8},{4,12},{8,16},{12,20},{16,24},{20,28},{1,9},{5,13},{9,17},{1... | collective-permute-start | bytes 3145736 | tf_op jit(solution)/shard_map/ppermute | solution.py:173
  95.0 32.7 %collective-permute-start.11 = (bf16[2,64,1792]{2,1,0:T(8,128)(2,1)}, bf16[2,64,1792]{2,1,0:T(8,128)(2,1)}, u32[]{:S(2)}, u32[]{:S(2)}) collective-permute-start(bf16[2,64,1792]{2,1,0:T(8,128)(2,1)} %dynamic-slice_bitcast_fusion.13), channel_id=1, source_target_pairs={{0,1},{1,0},{2,3},{3,2},{4,5},{5,4},{6,7},{7,6},{8,9},{9,8},{10,11... | collective-permute-start | bytes 1376264 | tf_op jit(solution)/shard_map/ppermute | solution.py:20
  112.5 13.5 %collective-permute-start.24 = (bf16[2,64,1792]{2,1,0:T(8,128)(2,1)S(1)}, bf16[2,64,1792]{2,1,0:T(8,128)(2,1)S(1)}, u32[]{:S(2)}, u32[]{:S(2)}) collective-permute-start(bf16[2,64,1792]{2,1,0:T(8,128)(2,1)S(1)} %dynamic-slice_bitcast_fusion.6), channel_id=1, source_target_pairs={{0,2},{1,3},{2,0},{3,1},{4,6},{5,7},{6,4},{7,5},{8,10},{9,11},{10,... | collective-permute-start | bytes 1376264 | tf_op jit(solution)/shard_map/ppermute | solution.py:20
  114.0 20.3 %collective-permute-start.12 = (bf16[2,64,1792]{2,1,0:T(8,128)(2,1)S(1)}, bf16[2,64,1792]{2,1,0:T(8,128)(2,1)S(1)}, u32[]{:S(2)}, u32[]{:S(2)}) collective-permute-start(bf16[2,64,1792]{2,1,0:T(8,128)(2,1)S(1)} %dynamic-slice_bitcast_fusion.12), channel_id=1, source_target_pairs={{0,2},{1,3},{2,0},{3,1},{4,6},{5,7},{6,4},{7,5},{8,10},{9,11},{10,... | collective-permute-start | bytes 1376264 | tf_op jit(solution)/shard_map/ppermute | solution.py:20
  140.1 13.9 %collective-permute-start.17 = (bf16[256,2048]{1,0:T(8,128)(2,1)S(1)}, bf16[256,2048]{1,0:T(8,128)(2,1)S(1)}, u32[]{:S(2)}, u32[]{:S(2)}) collective-permute-start(bf16[256,2048]{1,0:T(8,128)(2,1)S(1)} %fusion.3.upper_ref.refs_4_), channel_id=1, source_target_pairs={{0,4},{4,0},{8,12},{12,8},{16,20},{20,16},{24,28},{28,24},{1,5},{5... | collective-permute-start | bytes 3145736 | tf_op jit(solution)/shard_map/ppermute | solution.py:20
  141.8 55.6 %collective-permute-start.18 = (bf16[256,2048]{1,0:T(8,128)(2,1)}, bf16[256,2048]{1,0:T(8,128)(2,1)}, u32[]{:S(2)}, u32[]{:S(2)}) collective-permute-start(bf16[256,2048]{1,0:T(8,128)(2,1)} %collective-permute-done.9), channel_id=1, source_target_pairs={{0,8},{4,12},{8,16},{12,20},{16,24},{20,28},{1,9},{5,13},{9,17},{1... | collective-permute-start | bytes 3145736 | tf_op jit(solution)/shard_map/ppermute | solution.py:173
  145.5 51.9 %collective-permute-start.19 = (bf16[256,2048]{1,0:T(8,128)(2,1)}, bf16[256,2048]{1,0:T(8,128)(2,1)}, u32[]{:S(2)}, u32[]{:S(2)}) collective-permute-start(bf16[256,2048]{1,0:T(8,128)(2,1)} %collective-permute-done.10), channel_id=1, source_target_pairs={{8,0},{12,4},{16,8},{20,12},{24,16},{28,20},{9,1},{13,5},{17,9},{2... | collective-permute-start | bytes 3145736 | tf_op jit(solution)/shard_map/ppermute | solution.py:174
  164.9 32.5 %collective-permute-start.20 = (bf16[2,64,1792]{2,1,0:T(8,128)(2,1)}, bf16[2,64,1792]{2,1,0:T(8,128)(2,1)}, u32[]{:S(2)}, u32[]{:S(2)}) collective-permute-start(bf16[2,64,1792]{2,1,0:T(8,128)(2,1)} %dynamic-slice_bitcast_fusion.9), channel_id=1, source_target_pairs={{0,1},{1,0},{2,3},{3,2},{4,5},{5,4},{6,7},{7,6},{8,9},{9,8},{10,11... | collective-permute-start | bytes 1376264 | tf_op jit(solution)/shard_map/ppermute | solution.py:20
  182.1 13.5 %collective-permute-start.29 = (bf16[2,64,1792]{2,1,0:T(8,128)(2,1)S(1)}, bf16[2,64,1792]{2,1,0:T(8,128)(2,1)S(1)}, u32[]{:S(2)}, u32[]{:S(2)}) collective-permute-start(bf16[2,64,1792]{2,1,0:T(8,128)(2,1)S(1)} %dynamic-slice_bitcast_fusion.4), channel_id=1, source_target_pairs={{0,2},{1,3},{2,0},{3,1},{4,6},{5,7},{6,4},{7,5},{8,10},{9,11},{10,... | collective-permute-start | bytes 1376264 | tf_op jit(solution)/shard_map/ppermute | solution.py:20
  183.6 20.3 %collective-permute-start.21 = (bf16[2,64,1792]{2,1,0:T(8,128)(2,1)S(1)}, bf16[2,64,1792]{2,1,0:T(8,128)(2,1)S(1)}, u32[]{:S(2)}, u32[]{:S(2)}) collective-permute-start(bf16[2,64,1792]{2,1,0:T(8,128)(2,1)S(1)} %dynamic-slice_bitcast_fusion.8), channel_id=1, source_target_pairs={{0,2},{1,3},{2,0},{3,1},{4,6},{5,7},{6,4},{7,5},{8,10},{9,11},{10,... | collective-permute-start | bytes 1376264 | tf_op jit(solution)/shard_map/ppermute | solution.py:20
  209.8 13.9 %collective-permute-start.26 = (bf16[256,2048]{1,0:T(8,128)(2,1)S(1)}, bf16[256,2048]{1,0:T(8,128)(2,1)S(1)}, u32[]{:S(2)}, u32[]{:S(2)}) collective-permute-start(bf16[256,2048]{1,0:T(8,128)(2,1)S(1)} %select_select_fusion.1.upper_ref.refs_6_), channel_id=1, source_target_pairs={{0,4},{4,0},{8,12},{12,8},{16,20},{20,16},{24,28},{28,24},{1,5},{5... | collective-permute-start | bytes 3145736 | tf_op jit(solution)/shard_map/ppermute | solution.py:20
  234.6 44.8 %collective-permute-start.39 = (bf16[2,64,1792]{2,1,0:T(8,128)(2,1)}, bf16[2,64,1792]{2,1,0:T(8,128)(2,1)}, u32[]{:S(2)}, u32[]{:S(2)}) collective-permute-start(bf16[2,64,1792]{2,1,0:T(8,128)(2,1)} %dynamic-slice_bitcast_fusion.3), channel_id=1, source_target_pairs={{0,1},{1,0},{2,3},{3,2},{4,5},{5,4},{6,7},{7,6},{8,9},{9,8},{10,11... | collective-permute-start | bytes 1376264 | tf_op jit(solution)/shard_map/ppermute | solution.py:20
  258.3 24.8 %collective-permute-start.42 = (bf16[2,64,1792]{2,1,0:T(8,128)(2,1)S(1)}, bf16[2,64,1792]{2,1,0:T(8,128)(2,1)S(1)}, u32[]{:S(2)}, u32[]{:S(2)}) collective-permute-start(bf16[2,64,1792]{2,1,0:T(8,128)(2,1)S(1)} %dynamic-slice_bitcast_fusion.1), channel_id=1, source_target_pairs={{0,2},{1,3},{2,0},{3,1},{4,6},{5,7},{6,4},{7,5},{8,10},{9,11},{10,... | collective-permute-start | bytes 1376264 | tf_op jit(solution)/shard_map/ppermute | solution.py:20
  259.9 21.6 %collective-permute-start.40 = (bf16[2,64,1792]{2,1,0:T(8,128)(2,1)S(1)}, bf16[2,64,1792]{2,1,0:T(8,128)(2,1)S(1)}, u32[]{:S(2)}, u32[]{:S(2)}) collective-permute-start(bf16[2,64,1792]{2,1,0:T(8,128)(2,1)S(1)} %dynamic-slice_bitcast_fusion.2), channel_id=1, source_target_pairs={{0,1},{1,0},{2,3},{3,2},{4,5},{5,4},{6,7},{7,6},{8,9},{9,8},{10,11... | collective-permute-start | bytes 1376264 | tf_op jit(solution)/shard_map/ppermute | solution.py:20
  262.4 13.2 %collective-permute-start.36 = (bf16[2,64,896]{2,1,0:T(8,128)(2,1)S(1)}, bf16[2,64,896]{2,1,0:T(8,128)(2,1)S(1)}, u32[]{:S(2)}, u32[]{:S(2)}) collective-permute-start(bf16[2,64,896]{2,1,0:T(8,128)(2,1)S(1)} %pad_maximum_fusion.17), channel_id=1, source_target_pairs={{0,2},{1,3},{2,0},{3,1},{4,6},{5,7},{6,4},{7,5},{8,10},{9,11},{10,... | collective-permute-start | bytes 688136 | tf_op jit(solution)/shard_map/ppermute | solution.py:20
  263.7 13.3 %collective-permute-start.38 = (bf16[2,64,896]{2,1,0:T(8,128)(2,1)S(1)}, bf16[2,64,896]{2,1,0:T(8,128)(2,1)S(1)}, u32[]{:S(2)}, u32[]{:S(2)}) collective-permute-start(bf16[2,64,896]{2,1,0:T(8,128)(2,1)S(1)} %pad_maximum_fusion.18), channel_id=1, source_target_pairs={{0,1},{1,0},{2,3},{3,2},{4,5},{5,4},{6,7},{7,6},{8,9},{9,8},{10,11... | collective-permute-start | bytes 688136 | tf_op jit(solution)/shard_map/ppermute | solution.py:20
  275.6 13.5 %collective-permute-start.43 = (bf16[2,64,1792]{2,1,0:T(8,128)(2,1)S(1)}, bf16[2,64,1792]{2,1,0:T(8,128)(2,1)S(1)}, u32[]{:S(2)}, u32[]{:S(2)}) collective-permute-start(bf16[2,64,1792]{2,1,0:T(8,128)(2,1)S(1)} %dynamic-slice_bitcast_fusion), channel_id=1, source_target_pairs={{0,2},{1,3},{2,0},{3,1},{4,6},{5,7},{6,4},{7,5},{8,10},{9,11},{10,... | collective-permute-start | bytes 1376264 | tf_op jit(solution)/shard_map/ppermute | solution.py:20
  276.9 21.9 %collective-permute-start.32 = (bf16[2,64,1792]{2,1,0:T(8,128)(2,1)S(1)}, bf16[2,64,1792]{2,1,0:T(8,128)(2,1)S(1)}, u32[]{:S(2)}, u32[]{:S(2)}) collective-permute-start(bf16[2,64,1792]{2,1,0:T(8,128)(2,1)S(1)} %pad_maximum_fusion.9), channel_id=1, source_target_pairs={{0,2},{1,3},{2,0},{3,1},{4,6},{5,7},{6,4},{7,5},{8,10},{9,11},{10,... | collective-permute-start | bytes 1376264 | tf_op jit(solution)/shard_map/ppermute | solution.py:20
  279.4 19.5 %collective-permute-start.34 = (bf16[2,64,1792]{2,1,0:T(8,128)(2,1)S(1)}, bf16[2,64,1792]{2,1,0:T(8,128)(2,1)S(1)}, u32[]{:S(2)}, u32[]{:S(2)}) collective-permute-start(bf16[2,64,1792]{2,1,0:T(8,128)(2,1)S(1)} %pad_maximum_fusion.10), channel_id=1, source_target_pairs={{0,1},{1,0},{2,3},{3,2},{4,5},{5,4},{6,7},{7,6},{8,9},{9,8},{10,11... | collective-permute-start | bytes 1376264 | tf_op jit(solution)/shard_map/ppermute | solution.py:20
  281.7 24.5 %collective-permute-start.41 = (bf16[64,3584]{1,0:T(8,128)(2,1)S(1)}, bf16[64,3584]{1,0:T(8,128)(2,1)S(1)}, u32[]{:S(2)}, u32[]{:S(2)}) collective-permute-start(bf16[64,3584]{1,0:T(8,128)(2,1)S(1)} %pad_maximum_fusion.13), channel_id=1, source_target_pairs={{0,2},{1,3},{2,0},{3,1},{4,6},{5,7},{6,4},{7,5},{8,10},{9,11},{10,... | collective-permute-start | bytes 1376264 | tf_op jit(solution)/shard_map/ppermute | solution.py:20
  289.2 17.0 %collective-permute-start.44 = (bf16[64,3584]{1,0:T(8,128)(2,1)S(1)}, bf16[64,3584]{1,0:T(8,128)(2,1)S(1)}, u32[]{:S(2)}, u32[]{:S(2)}) collective-permute-start(bf16[64,3584]{1,0:T(8,128)(2,1)S(1)} %pad_maximum_fusion.14), channel_id=1, source_target_pairs={{0,1},{1,0},{2,3},{3,2},{4,5},{5,4},{6,7},{7,6},{8,9},{9,8},{10,11... | collective-permute-start | bytes 1376264 | tf_op jit(solution)/shard_map/ppermute | solution.py:20
  (60 other events, 803.5 us)
